TPU v7x, 512 devices: a whole 4x8x8 slice. The times are simulated.
512 devices in a mesh: gx: 64 (over z_lo, x, y), gy: 8 (over z_hi, core).
Axes of the slice: x: 4, y: 8, z: 8 (z_hi: 4, z_lo: 2; z = z_hi * 2 + z_lo), core: 2. Of those that a mesh axis runs over, the one named last changes fastest.
Arguments:
- position: float32 [3, 2097152], P(None, ('gx', 'gy')), may hold values from 0.05 to 0.95, as said below
- momentum: float32 [3, 2097152], P(None, ('gx', 'gy')), may hold values from -1.6 to 1.6, as said below
- cell_first: int32 [3, 2097152], P(None, ('gx', 'gy')), may hold values from 0 to 255, as said below
- cell_second: int32 [3, 2097152], P(None, ('gx', 'gy')), may hold values from 0 to 255, as said below
- destination: int32 [2097152], P(('gx', 'gy')), may hold values from 0 to 4, as said below
- slot_index: int32 [2097152], P(('gx', 'gy')), may hold values from 0 to 4095, as said below
- pull_position: float32 [3, 2097152], P(None, ('gx', 'gy')), may hold values from -6 to 6
- pull_momentum: float32 [3, 2097152], P(None, ('gx', 'gy')), may hold values from -6 to 6
Outputs:
- grad_position: float32 [3, 2097152], P(None, ('gx', 'gy'))
- grad_momentum: float32 [3, 2097152], P(None, ('gx', 'gy'))
Inputs may be any that keep to these rules, and one draw needn't show every extreme that they name: `destination`: 0: the particle stays on its device; 1 and 2: it moves to the next and to the previous device along gx; 3 and 4: to the next and to the previous device along gy (both axes wrap). From the particles of one device at most 256 go to each of its four neighbours, and in every draw some device sends exactly 256 to one neighbour. Between two neighbouring devices as many particles move one way as the other. A particle that moves to the next (previous) device along an axis lies in the last (first) cell layer of its device along that axis in cell_first. Over all particles the destination device and slot_index fill every index of every device exactly once. `cell_first`: the first component is below 2, the second below 8, the third below 256. `cell_second`: the cell_first of the particle that lands at this index, moved with it: a particle moving along gx goes from the last layer to the first or from the first to the last, likewise along gy; other components stay. The first component is below 2, the second below 8, the third below 256. `position`: A particle's drift_one leaves its cell along an axis exactly where destination sends it across that axis, in that direction. `momentum`: momenta of particles that move carry them across the cell face toward their destination.
All inputs are finite; a program needn't handle non-finite values.
Results may differ from a plain program's by a relative error of at most 0.000058.
Values sent between devices are 32-bit elements; how exact they have to be, the bound alone decides.
No kernel may reach another device: no remote copies, remote signals or barrier semaphores. Data moves between devices by JAX's collectives and lax.ppermute only.
A program may use at most 64 MiB of HBM per device.

v0:
```python
import jax
import jax.numpy as jnp
from jax import lax
from jax.sharding import PartitionSpec as P

CX = 2
CY = 8
NZ = 256
MOVE_MOST = 256
highest = lax.Precision.HIGHEST
step_size = 0.25
strength = 0.02


def with_halo(x, sides, width):
    for axis, dim in sides:
        peers, length = (lax.axis_size(axis), x.shape[dim])
        up = [(i, (i + 1) % peers) for i in range(peers)]
        down = [(j, i) for i, j in up]
        last = lax.slice_in_dim(x, length - width, length, axis=dim)
        first = lax.slice_in_dim(x, 0, width, axis=dim)
        before = lax.ppermute(last, axis, up)
        after = lax.ppermute(first, axis, down)
        x = jnp.concatenate([before, x, after], axis=dim)
    return x


def kernel_block(targets, sources, extent, reach_cells):
    distance = jnp.abs(targets[:, None] - sources[None, :])
    distance = jnp.minimum(distance, extent - distance)
    return jnp.exp(-distance.astype(jnp.float32) / reach_cells)


def cloud_weights(cell_block, frac_block, plane_count, row_count, depth_cells):
    index_row = jnp.arange(row_count, dtype=jnp.int32)[:, None]
    corner = (cell_block[1] * plane_count + cell_block[0])[None, :]
    hit_base = (index_row == corner).astype(jnp.float32)
    hit_east = (index_row == corner + 1).astype(jnp.float32)
    hit_north = (index_row == corner + plane_count).astype(jnp.float32)
    hit_both = (index_row == corner + plane_count + 1).astype(jnp.float32)
    west_weight = (1.0 - frac_block[0])[None, :]
    east_weight = frac_block[0][None, :]
    south_weight = (1.0 - frac_block[1])[None, :]
    north_weight = frac_block[1][None, :]
    planar = (
        hit_base * (west_weight * south_weight)
        + hit_east * (east_weight * south_weight)
        + hit_north * (west_weight * north_weight)
        + hit_both * (east_weight * north_weight)
    )
    slope_east = (hit_east - hit_base) * south_weight + (hit_both - hit_north) * north_weight
    slope_north = (hit_north - hit_base) * west_weight + (hit_both - hit_east) * east_weight
    index_depth = jnp.arange(depth_cells, dtype=jnp.int32)[:, None]
    lower_hit = (index_depth == cell_block[2][None, :]).astype(jnp.float32)
    upper_hit = (index_depth == ((cell_block[2] + 1) % depth_cells)[None, :]).astype(jnp.float32)
    vertical = lower_hit * (1.0 - frac_block[2])[None, :] + upper_hit * frac_block[2][None, :]
    slope_up = upper_hit - lower_hit
    return (planar, slope_east, slope_north, vertical, slope_up)


def particle_blocks(values):
    particle_count = values.shape[1]
    block_width = min(512, particle_count)
    return values.reshape(values.shape[0], particle_count // block_width, block_width).transpose(
        1, 0, 2
    )


def deposit(scales, cell_ids, offsets):
    layers = scales.shape[0]
    row_count = (CY + 1) * (CX + 1)

    def add_block(running, pieces):
        cell_block, frac_block, scale_block = pieces
        weights = cloud_weights(cell_block, frac_block, CX + 1, row_count, NZ)
        spread = scale_block[:, None, :] * weights[0][None]
        return (running + jnp.einsum("crb,zb->crz", spread, weights[3], precision=highest), None)

    initial = jnp.zeros((layers, row_count, NZ), jnp.float32)
    running, unused = lax.scan(
        add_block,
        initial,
        (particle_blocks(cell_ids), particle_blocks(offsets), particle_blocks(scales)),
    )
    return running.reshape(layers, CY + 1, CX + 1, NZ)


def sample_fields(fields, cell_ids, offsets, slopes):
    layers = fields.shape[0]
    row_count = fields.shape[1] * fields.shape[2]
    flattened = fields.reshape(layers * row_count, NZ)

    def one_block(pieces):
        cell_block, frac_block = pieces
        block_width = cell_block.shape[1]
        weights = cloud_weights(cell_block, frac_block, fields.shape[2], row_count, NZ)
        columns = jnp.concatenate([weights[3], weights[4]], 1) if slopes else weights[3]
        contracted = jnp.dot(
            flattened, columns, precision=highest, preferred_element_type=jnp.float32
        )
        contracted = contracted.reshape(layers, row_count, -1)
        nearby = contracted[:, :, :block_width]
        results = [jnp.sum(nearby * weights[0][None], axis=1)]
        if slopes:
            results.append(jnp.sum(nearby * weights[1][None], axis=1))
            results.append(jnp.sum(nearby * weights[2][None], axis=1))
            results.append(jnp.sum(contracted[:, :, block_width:] * weights[0][None], axis=1))
        return jnp.stack(results, 0)

    blocked = lax.map(one_block, (particle_blocks(cell_ids), particle_blocks(offsets)))
    return blocked.transpose(1, 2, 0, 3).reshape(blocked.shape[1], layers, cell_ids.shape[1])


def fold_planes(slab):
    planes = slab.shape[2]
    widened = with_halo(slab, (("gx", 2),), 2)
    return jnp.concatenate(
        [
            widened[:, :, 0:1],
            widened[:, :, 1:2] + widened[:, :, 2:3],
            widened[:, :, 3 : planes + 1],
            widened[:, :, planes + 1 : planes + 2] + widened[:, :, planes + 2 : planes + 3],
            widened[:, :, planes + 3 : planes + 4],
        ],
        axis=2,
    )


def smooth_depth(field):
    depth_cells = field.shape[-1]
    axis_cells = jnp.arange(depth_cells, dtype=jnp.int32)
    matrix = kernel_block(axis_cells, axis_cells, depth_cells, depth_cells / 16.0)
    return jnp.dot(
        field.reshape(-1, depth_cells),
        matrix,
        precision=highest,
        preferred_element_type=jnp.float32,
    ).reshape(field.shape)


def sum_lines(field):
    members = lax.axis_size("gy")
    band_rows = field.shape[1]
    own_rows = band_rows - 1
    extent = own_rows * members
    reach_cells = extent / 4.0
    anchor = lax.axis_index("gy") * own_rows
    targets = (anchor + jnp.arange(-1, own_rows + 2, dtype=jnp.int32)) % extent
    initial = jnp.zeros((field.shape[0], own_rows + 3, field.shape[2], field.shape[3]), jnp.float32)
    gathered = lax.all_gather(field, "gy", axis=1, tiled=True)
    length = gathered.shape[1]
    positions = jnp.arange(length, dtype=jnp.int32)
    sources = (positions // band_rows * own_rows + positions % band_rows) % extent
    weights = kernel_block(targets, sources, extent, reach_cells)
    return initial + jnp.einsum("ab,cbxz->caxz", weights, gathered, precision=highest)


def force_field(density):
    potential = sum_lines(smooth_depth(fold_planes(density)))
    potential = strength * potential
    centre = potential[:, 1:-1, 1:-1]
    push_east = -0.5 * (potential[:, 1:-1, 2:] - potential[:, 1:-1, :-2])
    push_north = -0.5 * (potential[:, 2:, 1:-1] - potential[:, :-2, 1:-1])
    push_up = -0.5 * (jnp.roll(centre, -1, 3) - jnp.roll(centre, 1, 3))
    return jnp.concatenate([push_east, push_north, push_up], 0)


def force_pullback(pushes, cell_ids, offsets, pull_force):
    folded = fold_planes(deposit(pull_force, cell_ids, offsets))
    across = 0.5 * (folded[0:1, :, 2:] - folded[0:1, :, :-2])
    upward = folded[2:3, :, 1:-1]
    across = across + 0.5 * (jnp.roll(upward, -1, 3) - jnp.roll(upward, 1, 3))
    line_sums = sum_lines(jnp.concatenate([across, folded[1:2, :, 1:-1]], 0))
    summed = line_sums[0:1, 1:-1] + 0.5 * (line_sums[1:2, 2:] - line_sums[1:2, :-2])
    density_pull = strength * smooth_depth(summed)
    sampled = sample_fields(jnp.concatenate([pushes, density_pull], 0), cell_ids, offsets, True)
    slopes = sampled[1:]
    return jnp.sum(slopes[:, :3] * pull_force[None], axis=1) + slopes[:, 3]


def pack_moves(destination, capacity):
    particle_count = destination.shape[0]
    grouped = jnp.argsort(destination, stable=True)
    group_size = jnp.sum(
        (destination[None, :] == jnp.arange(5, dtype=jnp.int32)[:, None]).astype(jnp.int32), axis=1
    )
    opening = jnp.cumsum(group_size) - group_size
    lane_index = jnp.arange(capacity, dtype=jnp.int32)
    chosen = jnp.stack(
        [
            grouped[jnp.minimum(opening[move_code] + lane_index, particle_count - 1)]
            for move_code in range(1, 5)
        ],
        0,
    )
    filled = lane_index[None, :] < group_size[1:5, None]
    return (chosen, filled)


def trade_pairs(outward_x, outward_y):
    widened_x = with_halo(outward_x, (("gx", 1),), 1)
    widened_y = with_halo(outward_y, (("gy", 1),), 1)
    return (widened_x[:, 0], widened_x[:, 3], widened_y[:, 0], widened_y[:, 3])


def local(
    position,
    momentum,
    cell_first,
    cell_second,
    destination,
    slot_index,
    pull_position,
    pull_momentum,
):
    particle_count = position.shape[1]
    unit_mass = jnp.ones((1, particle_count), jnp.float32)
    drift_one = position + step_size * momentum
    push_one = force_field(deposit(unit_mass, cell_first, drift_one))
    kick_one = momentum + step_size * sample_fields(push_one, cell_first, drift_one, False)[0]
    eastward = (destination == 1).astype(jnp.float32) - (destination == 2).astype(jnp.float32)
    northward = (destination == 3).astype(jnp.float32) - (destination == 4).astype(jnp.float32)
    shift_cells = jnp.stack([eastward, northward, jnp.zeros_like(eastward)], 0)
    payload = jnp.concatenate([drift_one - shift_cells, kick_one], 0)
    chosen, filled = pack_moves(destination, MOVE_MOST)
    slot_marks = jnp.where(filled, slot_index[chosen], particle_count).astype(jnp.float32)
    parcel = jnp.where(filled[None], payload[:, chosen], 0.0)
    parcel = jnp.concatenate([parcel, slot_marks[None]], 0)
    arrivals = trade_pairs(
        jnp.stack([parcel[:, 1], parcel[:, 0]], 1), jnp.stack([parcel[:, 3], parcel[:, 2]], 1)
    )
    arrivals = jnp.concatenate(arrivals, 1)
    received = arrivals[6].astype(jnp.int32)
    staying = jnp.where(destination == 0, slot_index, particle_count)
    placed = jnp.concatenate([staying, received], 0)
    arrived = (
        jnp.zeros((6, particle_count), jnp.float32)
        .at[:, placed]
        .set(jnp.concatenate([payload, arrivals[:6]], 1), mode="drop")
    )
    drift_two = arrived[:3] + step_size * arrived[3:]
    push_two = force_field(deposit(unit_mass, cell_second, drift_two))
    grad_drift_two = pull_position + force_pullback(
        push_two, cell_second, drift_two, step_size * pull_momentum
    )
    grad_kick_two = pull_momentum + step_size * grad_drift_two
    returning = jnp.concatenate([grad_drift_two, grad_kick_two], 0)
    sent_back = jnp.where(
        received[None] < particle_count,
        returning[:, jnp.minimum(received, particle_count - 1)],
        0.0,
    )
    sent_back = sent_back.reshape(6, 4, MOVE_MOST)
    homecoming = trade_pairs(sent_back[:, 0:2], sent_back[:, 2:4])
    returned = jnp.stack([homecoming[1], homecoming[0], homecoming[3], homecoming[2]], 1)
    gathered_home = jnp.where(destination[None] == 0, returning[:, slot_index], 0.0)
    home_spots = jnp.where(filled, chosen, particle_count).reshape(-1)
    gathered_home = gathered_home.at[:, home_spots].set(returned.reshape(6, -1), mode="drop")
    grad_drift_one = gathered_home[:3] + force_pullback(
        push_one, cell_first, drift_one, step_size * gathered_home[3:]
    )
    grad_momentum = gathered_home[3:] + step_size * grad_drift_one
    return (grad_drift_one, grad_momentum)


def solution(mesh):
    return jax.shard_map(
        local,
        mesh=mesh,
        in_specs=(
            P(None, ("gx", "gy")),
            P(None, ("gx", "gy")),
            P(None, ("gx", "gy")),
            P(None, ("gx", "gy")),
            P(("gx", "gy")),
            P(("gx", "gy")),
            P(None, ("gx", "gy")),
            P(None, ("gx", "gy")),
        ),
        out_specs=(P(None, ("gx", "gy")), P(None, ("gx", "gy"))),
        check_vma=False,
    )
```

profile of v0, /device:TPU:1, one launch (start us, length us, event | category | flops | bytes accessed | tf_op | source)
XLA Modules:
  0.0 329.3 jit_solution(1960830378543347206)
XLA Ops:
  1.4 1.0 maximum_subtract_fusion
  2.4 12.2 %while.91 = (s32[]{:T(128)}, f32[1,27,256]{2,1,0:T(8,128)S(1)}, s32[8,3,512]{2,1,0:T(4,128)}, f32[8,3,512]{2,1,0:T(4,128)S(1)}, s32[]{:T(128)}, /*index=5*/s32[]{:T(128)}, s32[]{}, s32[]{}) while((s32[]{:T(128)}, f32[1,27,256]{2,1,0:T(8,128)S(1)}, s32[8,3,512]{2,1,0:T(4,128)}, f32[8,3,512]{2,1,0:T(4,128)S(1)}, s32[]{:T(128)}, ...), condition=%wide.region_2.3_spmd.clone, body=%wide.region_1.2_spmd.clone.sunk | while | flops 43300868 | bytes 131215 | solution.py:80
  2.5 0.8 dynamic-slice_add_fusion.17
  4.0 0.8 dynamic-slice_add_fusion.17
  5.5 0.8 dynamic-slice_add_fusion.17
  7.0 0.8 dynamic-slice_add_fusion.17
  8.5 0.8 dynamic-slice_add_fusion.17
  10.1 0.8 dynamic-slice_add_fusion.17
  11.6 0.8 dynamic-slice_add_fusion.17
  13.1 0.8 dynamic-slice_add_fusion.17
  14.7 4.0 %collective-permute-start = (f32[1,9,2,256]{3,1,2,0:T(8,128)S(1)}, f32[1,9,2,256]{3,1,2,0:T(8,128)S(1)}, u32[]{:S(2)}, u32[]{:S(2)}) collective-permute-start(f32[1,9,2,256]{3,1,2,0:T(8,128)S(1)} %copy.330), channel_id=1, source_target_pairs={{0,8},{8,16},{16,24},{24,32},{32,40},{40,48},{48,56},{56,64},{64,7... | collective-permute-start | bytes 55304 | tf_op jit(solution)/shard_map/ppermute | solution.py:22
  18.7 7.8 %collective-permute-start.1 = (f32[1,9,2,256]{3,1,2,0:T(8,128)S(1)}, f32[1,9,2,256]{3,1,2,0:T(8,128)S(1)}, u32[]{:S(2)}, u32[]{:S(2)}) collective-permute-start(f32[1,9,2,256]{3,1,2,0:T(8,128)S(1)} %copy.334), channel_id=1, source_target_pairs={{8,0},{16,8},{24,16},{32,24},{40,32},{48,40},{56,48},{64,56},{72,6... | collective-permute-start | bytes 55304 | tf_op jit(solution)/shard_map/ppermute | solution.py:23
  28.9 5.8 %sort.17 = (s32[4096]{0:T(1024)}, s32[4096]{0:T(1024)S(1)}) sort(s32[4096]{0:T(1024)S(1)} %copy-done.3, s32[4096]{0:T(1024)S(1)} %iota.429), dimensions={0}, to_apply=%region_6.7 | sort | flops 49152 | bytes 65536 | tf_op jit(solution)/shard_map/jit(argsort)/sort | solution.py:183
  34.7 1.7 gather_fusion
  36.4 1.7 gather_fusion.1
  39.5 1.7 gather_fusion.2
  41.2 1.7 gather_fusion.3
  43.1 6.2 %gather_fusion.5 = s32[1024]{0:T(1024)S(1)} fusion(s32[4096]{0:T(1024)S(1)} %copy-done, s32[1024]{0:T(1024)S(1)} %broadcast_clamp_fusion.1), kind=kCustom, calls=%fused_computation.5 | custom fusion | bytes 12288 | tf_op jit(solution)/shard_map/gather | solution.py:226
  49.9 20.6 %all-gather = f32[72,5,256]{2,1,0:T(8,128)S(1)} all-gather(f32[9,5,256]{2,1,0:T(8,128)S(1)} %fusion.143), channel_id=2, replica_groups=mesh['gx'=64,'gy'=8] {'gy'}, dimensions={0}, use_global_device_ids=true | all-gather | bytes 414720 | tf_op jit(solution)/shard_map/all_gather | solution.py:150
  71.4 13.0 %while.88 = (s32[]{:T(128)}, f32[8,1,3,512]{3,2,1,0:T(4,128)S(1)}, s32[8,3,512]{2,1,0:T(4,128)}, f32[8,3,512]{2,1,0:T(4,128)S(1)}, f32[81,256]{1,0:T(8,128)S(1)}, /*index=5*/s32[]{:T(128)}, s32[]{:T(128)}, s32[]{}, s32[]{}) while((s32[]{:T(128)}, f32[8,1,3,512]{3,2,1,0:T(4,128)S(1)}, s32[8,3,512]{2,1,0:T(4,128)}, f32[8,3,512]{2,1,0:T(4,128)S(1)}, ...), condition=%wide.region_5.6_spmd, body=%wide.region_3.5_spmd.sunk | while | flops 128303104 | bytes 955537 | solution.py:110
  71.4 0.8 dynamic-slice_add_fusion.14
  73.0 0.8 dynamic-slice_add_fusion.14
  76.3 0.8 dynamic-slice_add_fusion.14
  81.1 0.8 dynamic-slice_add_fusion.14
  85.1 2.8 gather_fusion.4
  88.1 2.1 collective-permute-start.5
  90.2 4.4 %collective-permute-start.4 = (f32[7,1,256]{2,1,0:T(1,128)S(1)}, f32[7,1,256]{2,1,0:T(1,128)S(1)}, u32[]{:S(2)}, u32[]{:S(2)}) collective-permute-start(f32[7,1,256]{2,1,0:T(1,128)S(1)} %get-tuple-element.759), channel_id=1, source_target_pairs={{0,1},{1,2},{2,3},{3,4},{4,5},{5,6},{6,7},{7,0},{8,9},{9,10},{10,1... | collective-permute-start | bytes 21512 | tf_op jit(solution)/shard_map/ppermute | solution.py:22
  94.6 4.4 %collective-permute-start.3 = (f32[7,1,256]{2,1,0:T(1,128)S(1)}, f32[7,1,256]{2,1,0:T(1,128)S(1)}, u32[]{:S(2)}, u32[]{:S(2)}) collective-permute-start(f32[7,1,256]{2,1,0:T(1,128)S(1)} %get-tuple-element.757), channel_id=1, source_target_pairs={{8,0},{16,8},{24,16},{32,24},{40,32},{48,40},{56,48},{64,56},{72,6... | collective-permute-start | bytes 21512 | tf_op jit(solution)/shard_map/ppermute | solution.py:23
  99.0 1.9 collective-permute-start.2
  101.0 6.6 %collective-permute-done.2 = f32[7,1,256]{2,1,0:T(1,128)S(1)} collective-permute-done((f32[7,1,256]{2,1,0:T(1,128)S(1)}, f32[7,1,256]{2,1,0:T(1,128)S(1)}, u32[]{:S(2)}, u32[]{:S(2)}) %collective-permute-start.2) | collective-permute-done | bytes 7200 | tf_op jit(solution)/shard_map/ppermute | solution.py:22
  107.7 2.2 copy.281
  109.9 14.1 %scatter_custom_fusion = f32[6,4096]{0,1:T(8,128)S(1)} fusion(s32[5120]{0:T(1024)S(1)} %bitcast.439, f32[5120,6]{1,0:T(8,128)} %copy.281, f32[]{:T(128)} %constant.571.clone.1), kind=kCustom, calls=%fused_computation.335 | custom fusion | bytes 98816 | tf_op jit(solution)/shard_map/scatter | solution.py:239
  124.0 2.6 fusion.253
  126.6 2.4 copy.335
  129.7 12.2 %while.92 = (s32[]{:T(128)}, f32[1,27,256]{2,1,0:T(8,128)S(1)}, s32[8,3,512]{2,1,0:T(4,128)}, f32[8,3,512]{2,1,0:T(4,128)S(1)}, s32[]{:T(128)}, /*index=5*/s32[]{:T(128)}, s32[]{}, s32[]{}) while((s32[]{:T(128)}, f32[1,27,256]{2,1,0:T(8,128)S(1)}, s32[8,3,512]{2,1,0:T(4,128)}, f32[8,3,512]{2,1,0:T(4,128)S(1)}, s32[]{:T(128)}, ...), condition=%wide.region_10.11_spmd.clone, body=%wide.region_9.10_spmd.clone.sunk | while | flops 43300868 | bytes 131215 | solution.py:80
  129.7 0.8 dynamic-slice_add_fusion.18
  131.2 0.8 dynamic-slice_add_fusion.18
  132.8 0.8 dynamic-slice_add_fusion.18
  134.3 0.8 dynamic-slice_add_fusion.18
  141.9 13.4 %while.93 = (s32[]{:T(128)}, f32[3,27,256]{2,1,0:T(8,128)S(1)}, f32[8,3,512]{2,1,0:T(4,128)S(1)}, s32[8,3,512]{2,1,0:T(4,128)}, f32[8,3,512]{2,1,0:T(4,128)S(1)}, /*index=5*/s32[]{:T(128)}, s32[]{:T(128)}, s32[]{}, s32[]{}) while((s32[]{:T(128)}, f32[3,27,256]{2,1,0:T(8,128)S(1)}, f32[8,3,512]{2,1,0:T(4,128)S(1)}, ...), condition=%wide.region_12.13_spmd.clone, body=%wide.region_11.12_spmd.clone.sunk | while | flops 128304640 | bytes 370843 | solution.py:80
  155.5 1.9 collective-permute-start.6
  157.4 7.6 %collective-permute-start.7 = (f32[1,9,2,256]{3,1,2,0:T(8,128)S(1)}, f32[1,9,2,256]{3,1,2,0:T(8,128)S(1)}, u32[]{:S(2)}, u32[]{:S(2)}) collective-permute-start(f32[1,9,2,256]{3,1,2,0:T(8,128)S(1)} %copy.341), channel_id=1, source_target_pairs={{8,0},{16,8},{24,16},{32,24},{40,32},{48,40},{56,48},{64,56},{72,6... | collective-permute-start | bytes 55304 | tf_op jit(solution)/shard_map/ppermute | solution.py:23
  165.0 1.9 collective-permute-start.9
  167.0 7.6 %collective-permute-start.8 = (f32[3,9,2,256]{3,1,2,0:T(8,128)S(1)}, f32[3,9,2,256]{3,1,2,0:T(8,128)S(1)}, u32[]{:S(2)}, u32[]{:S(2)}) collective-permute-start(f32[3,9,2,256]{3,1,2,0:T(8,128)S(1)} %copy.344), channel_id=1, source_target_pairs={{8,0},{16,8},{24,16},{32,24},{40,32},{48,40},{56,48},{64,56},{72,6... | collective-permute-start | bytes 165896 | tf_op jit(solution)/shard_map/ppermute | solution.py:23
  175.1 18.5 %all-gather.1 = f32[72,5,256]{2,1,0:T(8,128)S(1)} all-gather(f32[9,5,256]{2,1,0:T(8,128)S(1)} %fusion.141), channel_id=3, replica_groups=mesh['gx'=64,'gy'=8] {'gy'}, dimensions={0}, use_global_device_ids=true | all-gather | bytes 414720 | tf_op jit(solution)/shard_map/all_gather | solution.py:150
  194.6 14.8 %all_gather.14 = f32[2,72,3,256]{3,0,2,1:T(2,128)S(1)} all-gather(f32[2,9,3,256]{3,0,2,1:T(2,128)S(1)} %copy.298), channel_id=1, replica_groups=mesh['gx'=64,'gy'=8] {'gy'}, dimensions={1}, use_global_device_ids=true | all-gather | bytes 497664 | tf_op jit(solution)/shard_map/all_gather | solution.py:150
  210.4 16.8 %while.89 = (s32[]{:T(128)}, f32[8,4,4,512]{3,2,1,0:T(4,128)S(1)}, s32[8,3,512]{2,1,0:T(4,128)}, f32[8,3,512]{2,1,0:T(4,128)S(1)}, f32[108,256]{1,0:T(8,128)S(1)}, /*index=5*/s32[]{:T(128)}, s32[]{:T(128)}, s32[]{}, s32[]{}) while((s32[]{:T(128)}, f32[8,4,4,512]{3,2,1,0:T(4,128)S(1)}, s32[8,3,512]{2,1,0:T(4,128)}, ...), condition=%wide.region_18.19_spmd, body=%wide.region_13.18_spmd.sunk | while | flops 341865984 | bytes 4495505 | solution.py:110
  228.2 2.8 gather_fusion.7
  231.3 2.3 collective-permute-start.10
  233.6 3.0 collective-permute-start.11
  236.6 2.6 collective-permute-start.12
  239.2 3.8 %collective-permute-start.13 = (f32[6,1,256]{2,1,0:T(1,128)S(1)}, f32[6,1,256]{2,1,0:T(1,128)S(1)}, u32[]{:S(2)}, u32[]{:S(2)}) collective-permute-start(f32[6,1,256]{2,1,0:T(1,128)S(1)} %get-tuple-element.771), channel_id=1, source_target_pairs={{0,1},{1,2},{2,3},{3,4},{4,5},{5,6},{6,7},{7,0},{8,9},{9,10},{10,1... | collective-permute-start | bytes 18440 | tf_op jit(solution)/shard_map/ppermute | solution.py:22
  243.0 14.1 %gather_fusion.6 = f32[4096,6]{1,0:T(8,128)} fusion(f32[6,4096]{0,1:T(8,128)S(1)} %copy.303, s32[4096]{0:T(1024)S(1)} %get-tuple-element.774), kind=kCustom, calls=%fused_computation.6 | custom fusion | bytes 212992 | tf_op jit(solution)/shard_map/gather | solution.py:256
  257.1 3.6 %select_bitcast_fusion = f32[6,4096]{0,1:T(8,128)S(1)} fusion(f32[4096,6]{1,0:T(8,128)} %gather_fusion.6, pred[4096]{0:T(1024)(128)(4,1)S(1)} %get-tuple-element.613), kind=kLoop, calls=%fused_computation.324 | loop fusion | flops 24576 | bytes 200704 | tf_op jit(solution)/shard_map/jit(_where)/select_n | solution.py:256
  261.0 4.1 %scatter_fusion = f32[6,4096]{0,1:T(8,128)S(1)} fusion(f32[6,4096]{0,1:T(8,128)S(1)} %select_bitcast_fusion, s32[1024]{0:T(1024)S(1)} %bitcast.440, f32[1024,6]{1,0:T(8,128)S(1)} %bitcast.355), kind=kCustom, calls=%fused_computation.9 | custom fusion | bytes 77824 | tf_op jit(solution)/shard_map/scatter | solution.py:258
  265.1 2.7 fusion.252
  267.8 2.2 copy.349
  270.1 13.4 %while.94 = (s32[]{:T(128)}, f32[3,27,256]{2,1,0:T(8,128)S(1)}, f32[8,3,512]{2,1,0:T(4,128)S(1)}, s32[8,3,512]{2,1,0:T(4,128)}, f32[8,3,512]{2,1,0:T(4,128)S(1)}, /*index=5*/s32[]{:T(128)}, s32[]{:T(128)}, s32[]{}, s32[]{}) while((s32[]{:T(128)}, f32[3,27,256]{2,1,0:T(8,128)S(1)}, f32[8,3,512]{2,1,0:T(4,128)S(1)}, ...), condition=%wide.region_22.23_spmd.clone, body=%wide.region_21.22_spmd.clone.sunk | while | flops 128304640 | bytes 370843 | solution.py:80
  270.1 0.9 dynamic-slice_add_fusion.20
  283.6 1.9 collective-permute-start.15
  285.6 7.6 %collective-permute-start.14 = (f32[3,9,2,256]{3,1,2,0:T(8,128)S(1)}, f32[3,9,2,256]{3,1,2,0:T(8,128)S(1)}, u32[]{:S(2)}, u32[]{:S(2)}) collective-permute-start(f32[3,9,2,256]{3,1,2,0:T(8,128)S(1)} %copy.352), channel_id=1, source_target_pairs={{8,0},{16,8},{24,16},{32,24},{40,32},{48,40},{56,48},{64,56},{72,6... | collective-permute-start | bytes 165896 | tf_op jit(solution)/shard_map/ppermute | solution.py:23
  294.3 1.2 collective-permute-done.14
  295.7 14.8 %all_gather.15 = f32[2,72,3,256]{3,0,2,1:T(2,128)S(1)} all-gather(f32[2,9,3,256]{3,0,2,1:T(2,128)S(1)} %copy.315), channel_id=1, replica_groups=mesh['gx'=64,'gy'=8] {'gy'}, dimensions={1}, use_global_device_ids=true | all-gather | bytes 497664 | tf_op jit(solution)/shard_map/all_gather | solution.py:150
  311.5 16.8 %while.90 = (s32[]{:T(128)}, f32[8,4,4,512]{3,2,1,0:T(4,128)S(1)}, s32[8,3,512]{2,1,0:T(4,128)}, f32[8,3,512]{2,1,0:T(4,128)S(1)}, f32[108,256]{1,0:T(8,128)S(1)}, /*index=5*/s32[]{:T(128)}, s32[]{:T(128)}, s32[]{}, s32[]{}) while((s32[]{:T(128)}, f32[8,4,4,512]{3,2,1,0:T(4,128)S(1)}, s32[8,3,512]{2,1,0:T(4,128)}, ...), condition=%wide.region_28.29_spmd, body=%wide.region_23.28_spmd.sunk | while | flops 341865984 | bytes 4495505 | solution.py:110
  (658 shorter events, 94.8 us)
Async XLA Ops:
  2.4 24.2 %copy-start.3 = (s32[4096]{0:T(1024)S(1)}, s32[4096]{0:T(1024)}, u32[]{:S(2)}) copy-start(s32[4096]{0:T(1024)} %param.26) | copy-start | bytes 49156
  14.7 34.8 %collective-permute-start = (f32[1,9,2,256]{3,1,2,0:T(8,128)S(1)}, f32[1,9,2,256]{3,1,2,0:T(8,128)S(1)}, u32[]{:S(2)}, u32[]{:S(2)}) collective-permute-start(f32[1,9,2,256]{3,1,2,0:T(8,128)S(1)} %copy.330), channel_id=1, source_target_pairs={{0,8},{8,16},{16,24},{24,32},{32,40},{40,48},{48,56},{56,64},{64,7... | collective-permute-start | bytes 55304 | tf_op jit(solution)/shard_map/ppermute | solution.py:22
  18.7 30.8 %collective-permute-start.1 = (f32[1,9,2,256]{3,1,2,0:T(8,128)S(1)}, f32[1,9,2,256]{3,1,2,0:T(8,128)S(1)}, u32[]{:S(2)}, u32[]{:S(2)}) collective-permute-start(f32[1,9,2,256]{3,1,2,0:T(8,128)S(1)} %copy.334), channel_id=1, source_target_pairs={{8,0},{16,8},{24,16},{32,24},{40,32},{48,40},{56,48},{64,56},{72,6... | collective-permute-start | bytes 55304 | tf_op jit(solution)/shard_map/ppermute | solution.py:23
  34.7 8.3 %copy-start = (s32[4096]{0:T(1024)S(1)}, s32[4096]{0:T(1024)}, u32[]{:S(2)}) copy-start(s32[4096]{0:T(1024)} %param.27) | copy-start | bytes 49156
  43.1 6.3 %copy-start.5 = (f32[3,4096]{1,0:T(4,128)S(1)}, f32[3,4096]{1,0:T(4,128)}, u32[]{:S(2)}) copy-start(f32[3,4096]{1,0:T(4,128)} %param.29) | copy-start | bytes 147460
  71.3 13.0 %copy-start.4 = (f32[3,4096]{1,0:T(4,128)S(1)}, f32[3,4096]{1,0:T(4,128)}, u32[]{:S(2)}) copy-start(f32[3,4096]{1,0:T(4,128)} %param.23) | copy-start | bytes 147460
  88.1 12.8 %collective-permute-start.5 = (f32[7,1,256]{2,1,0:T(1,128)S(1)}, f32[7,1,256]{2,1,0:T(1,128)S(1)}, u32[]{:S(2)}, u32[]{:S(2)}) collective-permute-start(f32[7,1,256]{2,1,0:T(1,128)S(1)} %get-tuple-element.758), channel_id=1, source_target_pairs={{1,0},{2,1},{3,2},{4,3},{5,4},{6,5},{7,6},{0,7},{9,8},{10,9},{11,1... | collective-permute-start | bytes 21512 | tf_op jit(solution)/shard_map/ppermute | solution.py:23
  90.2 10.8 %collective-permute-start.4 = (f32[7,1,256]{2,1,0:T(1,128)S(1)}, f32[7,1,256]{2,1,0:T(1,128)S(1)}, u32[]{:S(2)}, u32[]{:S(2)}) collective-permute-start(f32[7,1,256]{2,1,0:T(1,128)S(1)} %get-tuple-element.759), channel_id=1, source_target_pairs={{0,1},{1,2},{2,3},{3,4},{4,5},{5,6},{6,7},{7,0},{8,9},{9,10},{10,1... | collective-permute-start | bytes 21512 | tf_op jit(solution)/shard_map/ppermute | solution.py:22
  94.6 6.4 %collective-permute-start.3 = (f32[7,1,256]{2,1,0:T(1,128)S(1)}, f32[7,1,256]{2,1,0:T(1,128)S(1)}, u32[]{:S(2)}, u32[]{:S(2)}) collective-permute-start(f32[7,1,256]{2,1,0:T(1,128)S(1)} %get-tuple-element.757), channel_id=1, source_target_pairs={{8,0},{16,8},{24,16},{32,24},{40,32},{48,40},{56,48},{64,56},{72,6... | collective-permute-start | bytes 21512 | tf_op jit(solution)/shard_map/ppermute | solution.py:23
  99.0 8.6 %collective-permute-start.2 = (f32[7,1,256]{2,1,0:T(1,128)S(1)}, f32[7,1,256]{2,1,0:T(1,128)S(1)}, u32[]{:S(2)}, u32[]{:S(2)}) collective-permute-start(f32[7,1,256]{2,1,0:T(1,128)S(1)} %get-tuple-element.756), channel_id=1, source_target_pairs={{0,8},{8,16},{16,24},{24,32},{32,40},{40,48},{48,56},{56,64},{64,7... | collective-permute-start | bytes 21512 | tf_op jit(solution)/shard_map/ppermute | solution.py:22
  126.6 2.4 copy-start.2
  155.5 19.1 %collective-permute-start.6 = (f32[1,9,2,256]{3,1,2,0:T(8,128)S(1)}, f32[1,9,2,256]{3,1,2,0:T(8,128)S(1)}, u32[]{:S(2)}, u32[]{:S(2)}) collective-permute-start(f32[1,9,2,256]{3,1,2,0:T(8,128)S(1)} %copy.337), channel_id=1, source_target_pairs={{0,8},{8,16},{16,24},{24,32},{32,40},{40,48},{48,56},{56,64},{64,7... | collective-permute-start | bytes 55304 | tf_op jit(solution)/shard_map/ppermute | solution.py:22
  157.4 17.2 %collective-permute-start.7 = (f32[1,9,2,256]{3,1,2,0:T(8,128)S(1)}, f32[1,9,2,256]{3,1,2,0:T(8,128)S(1)}, u32[]{:S(2)}, u32[]{:S(2)}) collective-permute-start(f32[1,9,2,256]{3,1,2,0:T(8,128)S(1)} %copy.341), channel_id=1, source_target_pairs={{8,0},{16,8},{24,16},{32,24},{40,32},{48,40},{56,48},{64,56},{72,6... | collective-permute-start | bytes 55304 | tf_op jit(solution)/shard_map/ppermute | solution.py:23
  165.0 29.2 %collective-permute-start.9 = (f32[3,9,2,256]{3,1,2,0:T(8,128)S(1)}, f32[3,9,2,256]{3,1,2,0:T(8,128)S(1)}, u32[]{:S(2)}, u32[]{:S(2)}) collective-permute-start(f32[3,9,2,256]{3,1,2,0:T(8,128)S(1)} %copy.345), channel_id=1, source_target_pairs={{0,8},{8,16},{16,24},{24,32},{32,40},{40,48},{48,56},{56,64},{64,7... | collective-permute-start | bytes 165896 | tf_op jit(solution)/shard_map/ppermute | solution.py:22
  167.0 27.3 %collective-permute-start.8 = (f32[3,9,2,256]{3,1,2,0:T(8,128)S(1)}, f32[3,9,2,256]{3,1,2,0:T(8,128)S(1)}, u32[]{:S(2)}, u32[]{:S(2)}) collective-permute-start(f32[3,9,2,256]{3,1,2,0:T(8,128)S(1)} %copy.344), channel_id=1, source_target_pairs={{8,0},{16,8},{24,16},{32,24},{40,32},{48,40},{56,48},{64,56},{72,6... | collective-permute-start | bytes 165896 | tf_op jit(solution)/shard_map/ppermute | solution.py:23
  210.4 17.1 %copy-start.6 = (f32[3,4096]{1,0:T(4,128)S(1)}, f32[3,4096]{1,0:T(4,128)}, u32[]{:S(2)}) copy-start(f32[3,4096]{1,0:T(4,128)} %param.28) | copy-start | bytes 147460
  231.3 29.5 %collective-permute-start.10 = (f32[6,1,256]{2,1,0:T(1,128)S(1)}, f32[6,1,256]{2,1,0:T(1,128)S(1)}, u32[]{:S(2)}, u32[]{:S(2)}) collective-permute-start(f32[6,1,256]{2,1,0:T(1,128)S(1)} %get-tuple-element.770), channel_id=1, source_target_pairs={{8,0},{16,8},{24,16},{32,24},{40,32},{48,40},{56,48},{64,56},{72,6... | collective-permute-start | bytes 18440 | tf_op jit(solution)/shard_map/ppermute | solution.py:23
  233.6 27.1 %collective-permute-start.11 = (f32[6,1,256]{2,1,0:T(1,128)S(1)}, f32[6,1,256]{2,1,0:T(1,128)S(1)}, u32[]{:S(2)}, u32[]{:S(2)}) collective-permute-start(f32[6,1,256]{2,1,0:T(1,128)S(1)} %get-tuple-element.773), channel_id=1, source_target_pairs={{0,8},{8,16},{16,24},{24,32},{32,40},{40,48},{48,56},{56,64},{64,7... | collective-permute-start | bytes 18440 | tf_op jit(solution)/shard_map/ppermute | solution.py:22
  236.6 24.2 %collective-permute-start.12 = (f32[6,1,256]{2,1,0:T(1,128)S(1)}, f32[6,1,256]{2,1,0:T(1,128)S(1)}, u32[]{:S(2)}, u32[]{:S(2)}) collective-permute-start(f32[6,1,256]{2,1,0:T(1,128)S(1)} %get-tuple-element.772), channel_id=1, source_target_pairs={{1,0},{2,1},{3,2},{4,3},{5,4},{6,5},{7,6},{0,7},{9,8},{10,9},{11,1... | collective-permute-start | bytes 18440 | tf_op jit(solution)/shard_map/ppermute | solution.py:23
  239.2 21.6 %collective-permute-start.13 = (f32[6,1,256]{2,1,0:T(1,128)S(1)}, f32[6,1,256]{2,1,0:T(1,128)S(1)}, u32[]{:S(2)}, u32[]{:S(2)}) collective-permute-start(f32[6,1,256]{2,1,0:T(1,128)S(1)} %get-tuple-element.771), channel_id=1, source_target_pairs={{0,1},{1,2},{2,3},{3,4},{4,5},{5,6},{6,7},{7,0},{8,9},{9,10},{10,1... | collective-permute-start | bytes 18440 | tf_op jit(solution)/shard_map/ppermute | solution.py:22
  270.1 23.1 %copy-start.1 = (f32[3,4096]{0,1:T(8,128)S(1)}, f32[3,4096]{0,1:T(8,128)}, u32[]{:S(2)}) copy-start(f32[3,4096]{0,1:T(8,128)} %get-tuple-element.718) | copy-start | bytes 147460
  283.6 10.7 %collective-permute-start.15 = (f32[3,9,2,256]{3,1,2,0:T(8,128)S(1)}, f32[3,9,2,256]{3,1,2,0:T(8,128)S(1)}, u32[]{:S(2)}, u32[]{:S(2)}) collective-permute-start(f32[3,9,2,256]{3,1,2,0:T(8,128)S(1)} %copy.353), channel_id=1, source_target_pairs={{0,8},{8,16},{16,24},{24,32},{32,40},{40,48},{48,56},{56,64},{64,7... | collective-permute-start | bytes 165896 | tf_op jit(solution)/shard_map/ppermute | solution.py:22
  285.6 9.9 %collective-permute-start.14 = (f32[3,9,2,256]{3,1,2,0:T(8,128)S(1)}, f32[3,9,2,256]{3,1,2,0:T(8,128)S(1)}, u32[]{:S(2)}, u32[]{:S(2)}) collective-permute-start(f32[3,9,2,256]{3,1,2,0:T(8,128)S(1)} %copy.352), channel_id=1, source_target_pairs={{8,0},{16,8},{24,16},{32,24},{40,32},{48,40},{56,48},{64,56},{72,6... | collective-permute-start | bytes 165896 | tf_op jit(solution)/shard_map/ppermute | solution.py:23
where the time goes:
time: 334 us; the launch traced here: 329 us
  other arithmetic  71.2 us (21%)
  local copies, waits for them, and re-layouts  70.9 us (21%)
  blocking collectives  68.8 us (21%)
  starting transfers between devices  64.9 us (19%)
  matrix products  39.7 us (12%)
  waiting for transfers between devices  8.22 us (2%)
  loops' own time  3.7 us (1%)
    all_gather x4, blocking collectives, sum_lines(): gathered = lax.all_gather(field, 'gy', axis=1, tiled=True)  68.8 us
    add x56, other arithmetic, cloud_weights(): corner = (cell_block[1] * plane_count + cell_block[0])[None, :]  46.3 us
    ppermute x8, starting transfers between devices, with_halo(): after = lax.ppermute(first, axis, down)  42 us
    ppermute x8, starting transfers between devices, with_halo(): before = lax.ppermute(last, axis, up)  22.9 us
    dot_general x32, matrix products, add_block(): jnp.einsum('crb,zb->crz', spread, weights[3], precision=highest)  20.9 us
    dot_general x24, matrix products, one_block(): jnp.dot(flattened, columns, precision=highest, preferred_element_type=jnp...  15.9 us
    scatter x1, local copies, waits for them, and re-layouts, local(): arrived = jnp.zeros((6, particle_count), jnp.float32).at[:, placed].set(j...  14.1 us
    gather x1, local copies, waits for them, and re-layouts, local(): returning[:, slot_index]  14.1 us
  transfers between devices with their start and end apart: 16, of which 3 were waited for; matrix products, arithmetic and copies ran while one was open for 13% of the time, Pallas kernels for 0%

commit v1 on v0

--- a/solution.py
+++ b/solution.py
@@ -10,6 +10,12 @@
 highest = lax.Precision.HIGHEST
 step_size = 0.25
 strength = 0.02
+
+
+def touch_trails(arr):
+    return jnp.concatenate(
+        jax.lax.all_to_all(jnp.stack([arr] * jax.lax.axis_size("gy"), 0), "gy", 0, 0), axis=1
+    )
 
 
 def with_halo(x, sides, width):
@@ -147,7 +153,7 @@
     anchor = lax.axis_index("gy") * own_rows
     targets = (anchor + jnp.arange(-1, own_rows + 2, dtype=jnp.int32)) % extent
     initial = jnp.zeros((field.shape[0], own_rows + 3, field.shape[2], field.shape[3]), jnp.float32)
-    gathered = lax.all_gather(field, "gy", axis=1, tiled=True)
+    gathered = touch_trails(field)
     length = gathered.shape[1]
     positions = jnp.arange(length, dtype=jnp.int32)
     sources = (positions // band_rows * own_rows + positions % band_rows) % extent

time: 334 us -> 349 us (1.045)
  the two profiles are of different devices: /device:TPU:1 before, /device:TPU:62 now
where the time goes in v1:
time: 349 us; the launch traced here: 344 us
  starting transfers between devices  81.7 us (23%)
  local copies, waits for them, and re-layouts  74.8 us (21%)
  waiting for transfers between devices  71.3 us (20%)
  other arithmetic  71.2 us (20%)
  matrix products  39.8 us (11%)
  loops' own time  3.7 us (1%)
    all_to_all x4, waiting for transfers between devices, touch_trails(): jax.lax.all_to_all(jnp.stack([arr] * jax.lax.axis_size('gy'), 0), 'gy', 0...  54.8 us
    add x56, other arithmetic, cloud_weights(): corner = (cell_block[1] * plane_count + cell_block[0])[None, :]  46.2 us
    ppermute x8, starting transfers between devices, with_halo(): before = lax.ppermute(last, axis, up)  43.8 us
    dot_general x32, matrix products, add_block(): jnp.einsum('crb,zb->crz', spread, weights[3], precision=highest)  20.9 us
    all_to_all x4, starting transfers between devices, touch_trails(): jax.lax.all_to_all(jnp.stack([arr] * jax.lax.axis_size('gy'), 0), 'gy', 0...  20.7 us
    ppermute x8, starting transfers between devices, with_halo(): after = lax.ppermute(first, axis, down)  17.2 us
    dot_general x24, matrix products, one_block(): jnp.dot(flattened, columns, precision=highest, preferred_element_type=jnp...  15.9 us
    ppermute x8, waiting for transfers between devices, with_halo(): after = lax.ppermute(first, axis, down)  14.2 us
  transfers between devices with their start and end apart: 20, of which 8 were waited for; matrix products, arithmetic and copies ran while one was open for 13% of the time, Pallas kernels for 0%

profile of v1, /device:TPU:62, one launch (start us, length us, event | category | flops | bytes accessed | tf_op | source)
XLA Modules:
  0.0 344.3 jit_solution(6864580903838198963)
XLA Ops:
  1.4 1.0 maximum_subtract_fusion
  2.4 12.2 %while.91 = (s32[]{:T(128)}, f32[1,27,256]{2,1,0:T(8,128)S(1)}, s32[8,3,512]{2,1,0:T(4,128)}, f32[8,3,512]{2,1,0:T(4,128)S(1)}, s32[]{:T(128)}, /*index=5*/s32[]{:T(128)}, s32[]{}, s32[]{}) while((s32[]{:T(128)}, f32[1,27,256]{2,1,0:T(8,128)S(1)}, s32[8,3,512]{2,1,0:T(4,128)}, f32[8,3,512]{2,1,0:T(4,128)S(1)}, s32[]{:T(128)}, ...), condition=%wide.region_2.3_spmd.clone, body=%wide.region_1.2_spmd.clone.sunk | while | flops 43300868 | bytes 131215 | solution.py:86
  2.5 0.8 dynamic-slice_add_fusion.17
  14.6 3.4 collective-permute-start
  18.0 2.4 collective-permute-start.1
  22.3 5.8 %sort.17 = (s32[4096]{0:T(1024)}, s32[4096]{0:T(1024)S(1)}) sort(s32[4096]{0:T(1024)S(1)} %copy-done.3, s32[4096]{0:T(1024)S(1)} %iota.429), dimensions={0}, to_apply=%region_6.7 | sort | flops 49152 | bytes 65536 | tf_op jit(solution)/shard_map/jit(argsort)/sort | solution.py:189
  28.7 1.7 gather_fusion
  30.4 1.7 gather_fusion.1
  32.8 1.7 gather_fusion.2
  35.2 1.7 gather_fusion.3
  37.1 6.2 %gather_fusion.5 = s32[1024]{0:T(1024)S(1)} fusion(s32[4096]{0:T(1024)S(1)} %copy-done, s32[1024]{0:T(1024)S(1)} %broadcast_clamp_fusion.1), kind=kCustom, calls=%fused_computation.5 | custom fusion | bytes 12288 | tf_op jit(solution)/shard_map/gather | solution.py:232
  44.0 0.9 stack.129
  44.9 10.3 %all-to-all-start = ((f32[8,1,9,5,256]{4,1,3,2,0:T(1,128)}), f32[8,1,9,5,256]{4,1,3,2,0:T(1,128)S(1)}, u32[]{:S(2)}, u32[]{:S(2)}) async-start(f32[8,1,9,5,256]{4,1,3,2,0:T(1,128)} %stack.129), calls=%async_computation | async-start | bytes 737280 | tf_op jit(solution)/shard_map/all_to_all | solution.py:17
  55.2 15.0 %all-to-all-done = f32[8,1,9,5,256]{4,1,3,2,0:T(1,128)S(1)} async-done(((f32[8,1,9,5,256]{4,1,3,2,0:T(1,128)}), f32[8,1,9,5,256]{4,1,3,2,0:T(1,128)S(1)}, u32[]{:S(2)}, u32[]{:S(2)}) %all-to-all-start) | async-done | bytes 368672 | tf_op jit(solution)/shard_map/all_to_all | solution.py:17
  71.1 13.0 %while.88 = (s32[]{:T(128)}, f32[8,1,3,512]{3,2,1,0:T(4,128)S(1)}, s32[8,3,512]{2,1,0:T(4,128)}, f32[8,3,512]{2,1,0:T(4,128)S(1)}, f32[81,256]{1,0:T(8,128)S(1)}, /*index=5*/s32[]{:T(128)}, s32[]{:T(128)}, s32[]{}, s32[]{}) while((s32[]{:T(128)}, f32[8,1,3,512]{3,2,1,0:T(4,128)S(1)}, s32[8,3,512]{2,1,0:T(4,128)}, f32[8,3,512]{2,1,0:T(4,128)S(1)}, ...), condition=%wide.region_5.6_spmd, body=%wide.region_3.5_spmd.sunk | while | flops 128303104 | bytes 955537 | solution.py:116
  77.7 0.8 dynamic-slice_add_fusion.14
  79.3 0.8 dynamic-slice_add_fusion.14
  80.9 0.8 dynamic-slice_add_fusion.14
  82.5 0.8 dynamic-slice_add_fusion.14
  84.8 2.8 gather_fusion.4
  87.9 1.9 collective-permute-start.5
  89.8 2.4 collective-permute-start.4
  92.2 3.3 collective-permute-start.3
  95.5 6.8 %collective-permute-start.2 = (f32[7,1,256]{2,1,0:T(1,128)S(1)}, f32[7,1,256]{2,1,0:T(1,128)S(1)}, u32[]{:S(2)}, u32[]{:S(2)}) collective-permute-start(f32[7,1,256]{2,1,0:T(1,128)S(1)} %get-tuple-element.766), channel_id=1, source_target_pairs={{0,8},{8,16},{16,24},{24,32},{32,40},{40,48},{48,56},{56,64},{64,7... | collective-permute-start | bytes 21512 | tf_op jit(solution)/shard_map/ppermute | solution.py:28
  102.4 1.2 collective-permute-done.2
  103.7 2.3 copy.298
  106.0 14.1 %scatter_custom_fusion = f32[6,4096]{0,1:T(8,128)S(1)} fusion(s32[5120]{0:T(1024)S(1)} %bitcast.455, f32[5120,6]{1,0:T(8,128)} %copy.298, f32[]{:T(128)} %constant.571.clone.1), kind=kCustom, calls=%fused_computation.335 | custom fusion | bytes 98816 | tf_op jit(solution)/shard_map/scatter | solution.py:245
  120.1 2.6 fusion.253
  122.7 2.4 copy.346
  125.7 13.3 %while.93 = (s32[]{:T(128)}, f32[3,27,256]{2,1,0:T(8,128)S(1)}, f32[8,3,512]{2,1,0:T(4,128)S(1)}, s32[8,3,512]{2,1,0:T(4,128)}, f32[8,3,512]{2,1,0:T(4,128)S(1)}, /*index=5*/s32[]{:T(128)}, s32[]{:T(128)}, s32[]{}, s32[]{}) while((s32[]{:T(128)}, f32[3,27,256]{2,1,0:T(8,128)S(1)}, f32[8,3,512]{2,1,0:T(4,128)S(1)}, ...), condition=%wide.region_12.13_spmd.clone, body=%wide.region_11.12_spmd.clone.sunk | while | flops 128304640 | bytes 370843 | solution.py:86
  125.8 0.8 dynamic-slice_add_fusion.19
  127.5 0.8 dynamic-slice_add_fusion.19
  139.3 12.2 %while.92 = (s32[]{:T(128)}, f32[1,27,256]{2,1,0:T(8,128)S(1)}, s32[8,3,512]{2,1,0:T(4,128)}, f32[8,3,512]{2,1,0:T(4,128)S(1)}, s32[]{:T(128)}, /*index=5*/s32[]{:T(128)}, s32[]{}, s32[]{}) while((s32[]{:T(128)}, f32[1,27,256]{2,1,0:T(8,128)S(1)}, s32[8,3,512]{2,1,0:T(4,128)}, f32[8,3,512]{2,1,0:T(4,128)S(1)}, s32[]{:T(128)}, ...), condition=%wide.region_10.11_spmd.clone, body=%wide.region_9.10_spmd.clone.sunk | while | flops 43300868 | bytes 131215 | solution.py:86
  151.5 8.4 %collective-permute-start.6 = (f32[1,9,2,256]{3,2,1,0:T(2,128)S(1)}, f32[1,9,2,256]{3,2,1,0:T(2,128)S(1)}, u32[]{:S(2)}, u32[]{:S(2)}) collective-permute-start(f32[1,9,2,256]{3,2,1,0:T(2,128)S(1)} %get-tuple-element.760), channel_id=1, source_target_pairs={{0,8},{8,16},{16,24},{24,32},{32,40},{40,48},{48,56},{56,64},{64,7... | collective-permute-start | bytes 55304 | tf_op jit(solution)/shard_map/ppermute | solution.py:28
  159.9 1.9 collective-permute-start.7
  161.9 8.1 %collective-permute-start.9 = (f32[3,9,2,256]{3,1,2,0:T(8,128)S(1)}, f32[3,9,2,256]{3,1,2,0:T(8,128)S(1)}, u32[]{:S(2)}, u32[]{:S(2)}) collective-permute-start(f32[3,9,2,256]{3,1,2,0:T(8,128)S(1)} %copy.351), channel_id=1, source_target_pairs={{0,8},{8,16},{16,24},{24,32},{32,40},{40,48},{48,56},{56,64},{64,7... | collective-permute-start | bytes 165896 | tf_op jit(solution)/shard_map/ppermute | solution.py:28
  170.0 1.9 collective-permute-start.8
  172.5 0.9 stack.135
  173.5 3.4 %all-to-all-start.1 = ((f32[8,1,9,5,256]{4,1,3,2,0:T(1,128)}), f32[8,1,9,5,256]{4,1,3,2,0:T(1,128)S(1)}, u32[]{:S(2)}, u32[]{:S(2)}) async-start(f32[8,1,9,5,256]{4,1,3,2,0:T(1,128)} %stack.135), calls=%async_computation.1 | async-start | bytes 737280 | tf_op jit(solution)/shard_map/all_to_all | solution.py:17
  176.9 3.9 %collective-permute-done.8 = f32[3,9,2,256]{3,1,2,0:T(8,128)S(1)} collective-permute-done((f32[3,9,2,256]{3,1,2,0:T(8,128)S(1)}, f32[3,9,2,256]{3,1,2,0:T(8,128)S(1)}, u32[]{:S(2)}, u32[]{:S(2)}) %collective-permute-start.8) | collective-permute-done | bytes 55328 | tf_op jit(solution)/shard_map/ppermute | solution.py:29
  181.2 10.7 %all-to-all-done.1 = f32[8,1,9,5,256]{4,1,3,2,0:T(1,128)S(1)} async-done(((f32[8,1,9,5,256]{4,1,3,2,0:T(1,128)}), f32[8,1,9,5,256]{4,1,3,2,0:T(1,128)S(1)}, u32[]{:S(2)}, u32[]{:S(2)}) %all-to-all-start.1) | async-done | bytes 368672 | tf_op jit(solution)/shard_map/all_to_all | solution.py:17
  191.9 0.9 stack.136
  192.7 3.5 %all-to-all-start.2 = ((f32[8,2,9,3,256]{4,1,3,2,0:T(2,128)}), f32[8,2,9,3,256]{4,1,3,2,0:T(2,128)S(1)}, u32[]{:S(2)}, u32[]{:S(2)}) async-start(f32[8,2,9,3,256]{4,1,3,2,0:T(2,128)} %stack.136), calls=%async_computation.2 | async-start | bytes 884736 | tf_op jit(solution)/shard_map/all_to_all | solution.py:17
  197.0 15.1 %all-to-all-done.2 = f32[8,2,9,3,256]{4,1,3,2,0:T(2,128)S(1)} async-done(((f32[8,2,9,3,256]{4,1,3,2,0:T(2,128)}), f32[8,2,9,3,256]{4,1,3,2,0:T(2,128)S(1)}, u32[]{:S(2)}, u32[]{:S(2)}) %all-to-all-start.2) | async-done | bytes 442400 | tf_op jit(solution)/shard_map/all_to_all | solution.py:17
  213.1 16.8 %while.89 = (s32[]{:T(128)}, f32[8,4,4,512]{3,2,1,0:T(4,128)S(1)}, s32[8,3,512]{2,1,0:T(4,128)}, f32[8,3,512]{2,1,0:T(4,128)S(1)}, f32[108,256]{1,0:T(8,128)S(1)}, /*index=5*/s32[]{:T(128)}, s32[]{:T(128)}, s32[]{}, s32[]{}) while((s32[]{:T(128)}, f32[8,4,4,512]{3,2,1,0:T(4,128)S(1)}, s32[8,3,512]{2,1,0:T(4,128)}, ...), condition=%wide.region_18.19_spmd, body=%wide.region_13.18_spmd.sunk | while | flops 341865984 | bytes 4495505 | solution.py:116
  230.9 2.8 gather_fusion.7
  234.0 1.9 collective-permute-start.10
  235.9 8.1 %collective-permute-start.11 = (f32[6,1,256]{2,1,0:T(1,128)S(1)}, f32[6,1,256]{2,1,0:T(1,128)S(1)}, u32[]{:S(2)}, u32[]{:S(2)}) collective-permute-start(f32[6,1,256]{2,1,0:T(1,128)S(1)} %get-tuple-element.773), channel_id=1, source_target_pairs={{0,8},{8,16},{16,24},{24,32},{32,40},{40,48},{48,56},{56,64},{64,7... | collective-permute-start | bytes 18440 | tf_op jit(solution)/shard_map/ppermute | solution.py:28
  244.0 1.9 collective-permute-start.12
  246.0 2.4 collective-permute-start.13
  248.4 14.1 %gather_fusion.6 = f32[4096,6]{1,0:T(8,128)} fusion(f32[6,4096]{0,1:T(8,128)S(1)} %copy.319, s32[4096]{0:T(1024)S(1)} %get-tuple-element.778), kind=kCustom, calls=%fused_computation.6 | custom fusion | bytes 212992 | tf_op jit(solution)/shard_map/gather | solution.py:262
  262.5 3.6 %select_bitcast_fusion = f32[6,4096]{0,1:T(8,128)S(1)} fusion(f32[4096,6]{1,0:T(8,128)} %gather_fusion.6, pred[4096]{0:T(1024)(128)(4,1)S(1)} %get-tuple-element.613), kind=kLoop, calls=%fused_computation.324 | loop fusion | flops 24576 | bytes 200704 | tf_op jit(solution)/shard_map/jit(_where)/select_n | solution.py:262
  266.4 4.1 %scatter_fusion = f32[6,4096]{0,1:T(8,128)S(1)} fusion(f32[6,4096]{0,1:T(8,128)S(1)} %select_bitcast_fusion, s32[1024]{0:T(1024)S(1)} %bitcast.456, f32[1024,6]{1,0:T(8,128)S(1)} %bitcast.371), kind=kCustom, calls=%fused_computation.9 | custom fusion | bytes 77824 | tf_op jit(solution)/shard_map/scatter | solution.py:264
  270.5 2.7 fusion.252
  273.2 2.2 copy.355
  275.4 13.4 %while.94 = (s32[]{:T(128)}, f32[3,27,256]{2,1,0:T(8,128)S(1)}, f32[8,3,512]{2,1,0:T(4,128)S(1)}, s32[8,3,512]{2,1,0:T(4,128)}, f32[8,3,512]{2,1,0:T(4,128)S(1)}, /*index=5*/s32[]{:T(128)}, s32[]{:T(128)}, s32[]{}, s32[]{}) while((s32[]{:T(128)}, f32[3,27,256]{2,1,0:T(8,128)S(1)}, f32[8,3,512]{2,1,0:T(4,128)S(1)}, ...), condition=%wide.region_22.23_spmd.clone, body=%wide.region_21.22_spmd.clone.sunk | while | flops 128304640 | bytes 370843 | solution.py:86
  288.9 4.1 %collective-permute-start.15 = (f32[3,9,2,256]{3,1,2,0:T(8,128)S(1)}, f32[3,9,2,256]{3,1,2,0:T(8,128)S(1)}, u32[]{:S(2)}, u32[]{:S(2)}) collective-permute-start(f32[3,9,2,256]{3,1,2,0:T(8,128)S(1)} %copy.359), channel_id=1, source_target_pairs={{0,8},{8,16},{16,24},{24,32},{32,40},{40,48},{48,56},{56,64},{64,7... | collective-permute-start | bytes 165896 | tf_op jit(solution)/shard_map/ppermute | solution.py:28
  293.0 1.9 collective-permute-start.14
  295.0 1.0 collective-permute-done.15
  296.0 10.3 %collective-permute-done.14 = f32[3,9,2,256]{3,1,2,0:T(8,128)S(1)} collective-permute-done((f32[3,9,2,256]{3,1,2,0:T(8,128)S(1)}, f32[3,9,2,256]{3,1,2,0:T(8,128)S(1)}, u32[]{:S(2)}, u32[]{:S(2)}) %collective-permute-start.14) | collective-permute-done | bytes 55328 | tf_op jit(solution)/shard_map/ppermute | solution.py:29
  306.6 0.9 stack.143
  307.5 3.5 %all-to-all-start.3 = ((f32[8,2,9,3,256]{4,1,3,2,0:T(2,128)}), f32[8,2,9,3,256]{4,1,3,2,0:T(2,128)S(1)}, u32[]{:S(2)}, u32[]{:S(2)}) async-start(f32[8,2,9,3,256]{4,1,3,2,0:T(2,128)} %stack.143), calls=%async_computation.3 | async-start | bytes 884736 | tf_op jit(solution)/shard_map/all_to_all | solution.py:17
  311.6 14.0 %all-to-all-done.3 = f32[8,2,9,3,256]{4,1,3,2,0:T(2,128)S(1)} async-done(((f32[8,2,9,3,256]{4,1,3,2,0:T(2,128)}), f32[8,2,9,3,256]{4,1,3,2,0:T(2,128)S(1)}, u32[]{:S(2)}, u32[]{:S(2)}) %all-to-all-start.3) | async-done | bytes 442400 | tf_op jit(solution)/shard_map/all_to_all | solution.py:17
  326.5 16.8 %while.90 = (s32[]{:T(128)}, f32[8,4,4,512]{3,2,1,0:T(4,128)S(1)}, s32[8,3,512]{2,1,0:T(4,128)}, f32[8,3,512]{2,1,0:T(4,128)S(1)}, f32[108,256]{1,0:T(8,128)S(1)}, /*index=5*/s32[]{:T(128)}, s32[]{:T(128)}, s32[]{}, s32[]{}) while((s32[]{:T(128)}, f32[8,4,4,512]{3,2,1,0:T(4,128)S(1)}, s32[8,3,512]{2,1,0:T(4,128)}, ...), condition=%wide.region_28.29_spmd, body=%wide.region_23.28_spmd.sunk | while | flops 341865984 | bytes 4495505 | solution.py:116
  (658 shorter events, 103.0 us)
Async XLA Ops:
  2.4 18.1 %copy-start.3 = (s32[4096]{0:T(1024)S(1)}, s32[4096]{0:T(1024)}, u32[]{:S(2)}) copy-start(s32[4096]{0:T(1024)} %param.26) | copy-start | bytes 49156
  14.6 28.8 %collective-permute-start = (f32[1,9,2,256]{3,2,1,0:T(2,128)S(1)}, f32[1,9,2,256]{3,2,1,0:T(2,128)S(1)}, u32[]{:S(2)}, u32[]{:S(2)}) collective-permute-start(f32[1,9,2,256]{3,2,1,0:T(2,128)S(1)} %get-tuple-element.765), channel_id=1, source_target_pairs={{0,8},{8,16},{16,24},{24,32},{32,40},{40,48},{48,56},{56,64},{64,7... | collective-permute-start | bytes 55304 | tf_op jit(solution)/shard_map/ppermute | solution.py:28
  18.0 25.4 %collective-permute-start.1 = (f32[1,9,2,256]{3,2,1,0:T(2,128)S(1)}, f32[1,9,2,256]{3,2,1,0:T(2,128)S(1)}, u32[]{:S(2)}, u32[]{:S(2)}) collective-permute-start(f32[1,9,2,256]{3,2,1,0:T(2,128)S(1)} %get-tuple-element.764), channel_id=1, source_target_pairs={{8,0},{16,8},{24,16},{32,24},{40,32},{48,40},{56,48},{64,56},{72,6... | collective-permute-start | bytes 55304 | tf_op jit(solution)/shard_map/ppermute | solution.py:29
  28.7 8.4 %copy-start = (s32[4096]{0:T(1024)S(1)}, s32[4096]{0:T(1024)}, u32[]{:S(2)}) copy-start(s32[4096]{0:T(1024)} %param.27) | copy-start | bytes 49156
  37.1 18.1 %copy-start.5 = (f32[3,4096]{1,0:T(4,128)S(1)}, f32[3,4096]{1,0:T(4,128)}, u32[]{:S(2)}) copy-start(f32[3,4096]{1,0:T(4,128)} %param.29) | copy-start | bytes 147460
  44.9 25.3 %all-to-all-start = ((f32[8,1,9,5,256]{4,1,3,2,0:T(1,128)}), f32[8,1,9,5,256]{4,1,3,2,0:T(1,128)S(1)}, u32[]{:S(2)}, u32[]{:S(2)}) async-start(f32[8,1,9,5,256]{4,1,3,2,0:T(1,128)} %stack.129), calls=%async_computation | async-start | bytes 737280 | tf_op jit(solution)/shard_map/all_to_all | solution.py:17
  71.1 13.0 %copy-start.4 = (f32[3,4096]{1,0:T(4,128)S(1)}, f32[3,4096]{1,0:T(4,128)}, u32[]{:S(2)}) copy-start(f32[3,4096]{1,0:T(4,128)} %param.23) | copy-start | bytes 147460
  87.9 14.5 %collective-permute-start.5 = (f32[7,1,256]{2,1,0:T(1,128)S(1)}, f32[7,1,256]{2,1,0:T(1,128)S(1)}, u32[]{:S(2)}, u32[]{:S(2)}) collective-permute-start(f32[7,1,256]{2,1,0:T(1,128)S(1)} %get-tuple-element.768), channel_id=1, source_target_pairs={{1,0},{2,1},{3,2},{4,3},{5,4},{6,5},{7,6},{0,7},{9,8},{10,9},{11,1... | collective-permute-start | bytes 21512 | tf_op jit(solution)/shard_map/ppermute | solution.py:29
  89.8 12.6 %collective-permute-start.4 = (f32[7,1,256]{2,1,0:T(1,128)S(1)}, f32[7,1,256]{2,1,0:T(1,128)S(1)}, u32[]{:S(2)}, u32[]{:S(2)}) collective-permute-start(f32[7,1,256]{2,1,0:T(1,128)S(1)} %get-tuple-element.769), channel_id=1, source_target_pairs={{0,1},{1,2},{2,3},{3,4},{4,5},{5,6},{6,7},{7,0},{8,9},{9,10},{10,1... | collective-permute-start | bytes 21512 | tf_op jit(solution)/shard_map/ppermute | solution.py:28
  92.2 10.2 %collective-permute-start.3 = (f32[7,1,256]{2,1,0:T(1,128)S(1)}, f32[7,1,256]{2,1,0:T(1,128)S(1)}, u32[]{:S(2)}, u32[]{:S(2)}) collective-permute-start(f32[7,1,256]{2,1,0:T(1,128)S(1)} %get-tuple-element.767), channel_id=1, source_target_pairs={{8,0},{16,8},{24,16},{32,24},{40,32},{48,40},{56,48},{64,56},{72,6... | collective-permute-start | bytes 21512 | tf_op jit(solution)/shard_map/ppermute | solution.py:29
  95.5 8.1 %collective-permute-start.2 = (f32[7,1,256]{2,1,0:T(1,128)S(1)}, f32[7,1,256]{2,1,0:T(1,128)S(1)}, u32[]{:S(2)}, u32[]{:S(2)}) collective-permute-start(f32[7,1,256]{2,1,0:T(1,128)S(1)} %get-tuple-element.766), channel_id=1, source_target_pairs={{0,8},{8,16},{16,24},{24,32},{32,40},{40,48},{48,56},{56,64},{64,7... | collective-permute-start | bytes 21512 | tf_op jit(solution)/shard_map/ppermute | solution.py:28
  122.7 2.4 copy-start.2
  151.5 20.5 %collective-permute-start.6 = (f32[1,9,2,256]{3,2,1,0:T(2,128)S(1)}, f32[1,9,2,256]{3,2,1,0:T(2,128)S(1)}, u32[]{:S(2)}, u32[]{:S(2)}) collective-permute-start(f32[1,9,2,256]{3,2,1,0:T(2,128)S(1)} %get-tuple-element.760), channel_id=1, source_target_pairs={{0,8},{8,16},{16,24},{24,32},{32,40},{40,48},{48,56},{56,64},{64,7... | collective-permute-start | bytes 55304 | tf_op jit(solution)/shard_map/ppermute | solution.py:28
  159.9 12.1 %collective-permute-start.7 = (f32[1,9,2,256]{3,2,1,0:T(2,128)S(1)}, f32[1,9,2,256]{3,2,1,0:T(2,128)S(1)}, u32[]{:S(2)}, u32[]{:S(2)}) collective-permute-start(f32[1,9,2,256]{3,2,1,0:T(2,128)S(1)} %get-tuple-element.759), channel_id=1, source_target_pairs={{8,0},{16,8},{24,16},{32,24},{40,32},{48,40},{56,48},{64,56},{72,6... | collective-permute-start | bytes 55304 | tf_op jit(solution)/shard_map/ppermute | solution.py:29
  161.9 15.0 %collective-permute-start.9 = (f32[3,9,2,256]{3,1,2,0:T(8,128)S(1)}, f32[3,9,2,256]{3,1,2,0:T(8,128)S(1)}, u32[]{:S(2)}, u32[]{:S(2)}) collective-permute-start(f32[3,9,2,256]{3,1,2,0:T(8,128)S(1)} %copy.351), channel_id=1, source_target_pairs={{0,8},{8,16},{16,24},{24,32},{32,40},{40,48},{48,56},{56,64},{64,7... | collective-permute-start | bytes 165896 | tf_op jit(solution)/shard_map/ppermute | solution.py:28
  170.0 10.8 %collective-permute-start.8 = (f32[3,9,2,256]{3,1,2,0:T(8,128)S(1)}, f32[3,9,2,256]{3,1,2,0:T(8,128)S(1)}, u32[]{:S(2)}, u32[]{:S(2)}) collective-permute-start(f32[3,9,2,256]{3,1,2,0:T(8,128)S(1)} %copy.350), channel_id=1, source_target_pairs={{8,0},{16,8},{24,16},{32,24},{40,32},{48,40},{56,48},{64,56},{72,6... | collective-permute-start | bytes 165896 | tf_op jit(solution)/shard_map/ppermute | solution.py:29
  173.5 18.4 %all-to-all-start.1 = ((f32[8,1,9,5,256]{4,1,3,2,0:T(1,128)}), f32[8,1,9,5,256]{4,1,3,2,0:T(1,128)S(1)}, u32[]{:S(2)}, u32[]{:S(2)}) async-start(f32[8,1,9,5,256]{4,1,3,2,0:T(1,128)} %stack.135), calls=%async_computation.1 | async-start | bytes 737280 | tf_op jit(solution)/shard_map/all_to_all | solution.py:17
  192.7 19.4 %all-to-all-start.2 = ((f32[8,2,9,3,256]{4,1,3,2,0:T(2,128)}), f32[8,2,9,3,256]{4,1,3,2,0:T(2,128)S(1)}, u32[]{:S(2)}, u32[]{:S(2)}) async-start(f32[8,2,9,3,256]{4,1,3,2,0:T(2,128)} %stack.136), calls=%async_computation.2 | async-start | bytes 884736 | tf_op jit(solution)/shard_map/all_to_all | solution.py:17
  213.1 17.1 %copy-start.6 = (f32[3,4096]{1,0:T(4,128)S(1)}, f32[3,4096]{1,0:T(4,128)}, u32[]{:S(2)}) copy-start(f32[3,4096]{1,0:T(4,128)} %param.28) | copy-start | bytes 147460
  234.0 32.1 %collective-permute-start.10 = (f32[6,1,256]{2,1,0:T(1,128)S(1)}, f32[6,1,256]{2,1,0:T(1,128)S(1)}, u32[]{:S(2)}, u32[]{:S(2)}) collective-permute-start(f32[6,1,256]{2,1,0:T(1,128)S(1)} %get-tuple-element.770), channel_id=1, source_target_pairs={{8,0},{16,8},{24,16},{32,24},{40,32},{48,40},{56,48},{64,56},{72,6... | collective-permute-start | bytes 18440 | tf_op jit(solution)/shard_map/ppermute | solution.py:29
  235.9 30.2 %collective-permute-start.11 = (f32[6,1,256]{2,1,0:T(1,128)S(1)}, f32[6,1,256]{2,1,0:T(1,128)S(1)}, u32[]{:S(2)}, u32[]{:S(2)}) collective-permute-start(f32[6,1,256]{2,1,0:T(1,128)S(1)} %get-tuple-element.773), channel_id=1, source_target_pairs={{0,8},{8,16},{16,24},{24,32},{32,40},{40,48},{48,56},{56,64},{64,7... | collective-permute-start | bytes 18440 | tf_op jit(solution)/shard_map/ppermute | solution.py:28
  244.0 22.1 %collective-permute-start.12 = (f32[6,1,256]{2,1,0:T(1,128)S(1)}, f32[6,1,256]{2,1,0:T(1,128)S(1)}, u32[]{:S(2)}, u32[]{:S(2)}) collective-permute-start(f32[6,1,256]{2,1,0:T(1,128)S(1)} %get-tuple-element.772), channel_id=1, source_target_pairs={{1,0},{2,1},{3,2},{4,3},{5,4},{6,5},{7,6},{0,7},{9,8},{10,9},{11,1... | collective-permute-start | bytes 18440 | tf_op jit(solution)/shard_map/ppermute | solution.py:29
  246.0 20.2 %collective-permute-start.13 = (f32[6,1,256]{2,1,0:T(1,128)S(1)}, f32[6,1,256]{2,1,0:T(1,128)S(1)}, u32[]{:S(2)}, u32[]{:S(2)}) collective-permute-start(f32[6,1,256]{2,1,0:T(1,128)S(1)} %get-tuple-element.771), channel_id=1, source_target_pairs={{0,1},{1,2},{2,3},{3,4},{4,5},{5,6},{6,7},{7,0},{8,9},{9,10},{10,1... | collective-permute-start | bytes 18440 | tf_op jit(solution)/shard_map/ppermute | solution.py:28
  288.8 22.2 %copy-start.1 = (f32[3,4096]{0,1:T(8,128)S(1)}, f32[3,4096]{0,1:T(8,128)}, u32[]{:S(2)}) copy-start(f32[3,4096]{0,1:T(8,128)} %get-tuple-element.718) | copy-start | bytes 147460
  288.9 7.1 %collective-permute-start.15 = (f32[3,9,2,256]{3,1,2,0:T(8,128)S(1)}, f32[3,9,2,256]{3,1,2,0:T(8,128)S(1)}, u32[]{:S(2)}, u32[]{:S(2)}) collective-permute-start(f32[3,9,2,256]{3,1,2,0:T(8,128)S(1)} %copy.359), channel_id=1, source_target_pairs={{0,8},{8,16},{16,24},{24,32},{32,40},{40,48},{48,56},{56,64},{64,7... | collective-permute-start | bytes 165896 | tf_op jit(solution)/shard_map/ppermute | solution.py:28
  293.0 13.2 %collective-permute-start.14 = (f32[3,9,2,256]{3,1,2,0:T(8,128)S(1)}, f32[3,9,2,256]{3,1,2,0:T(8,128)S(1)}, u32[]{:S(2)}, u32[]{:S(2)}) collective-permute-start(f32[3,9,2,256]{3,1,2,0:T(8,128)S(1)} %copy.358), channel_id=1, source_target_pairs={{8,0},{16,8},{24,16},{32,24},{40,32},{48,40},{56,48},{64,56},{72,6... | collective-permute-start | bytes 165896 | tf_op jit(solution)/shard_map/ppermute | solution.py:29
  307.5 18.1 %all-to-all-start.3 = ((f32[8,2,9,3,256]{4,1,3,2,0:T(2,128)}), f32[8,2,9,3,256]{4,1,3,2,0:T(2,128)S(1)}, u32[]{:S(2)}, u32[]{:S(2)}) async-start(f32[8,2,9,3,256]{4,1,3,2,0:T(2,128)} %stack.143), calls=%async_computation.3 | async-start | bytes 884736 | tf_op jit(solution)/shard_map/all_to_all | solution.py:17
